TPU v7x, 32 devices: a whole 2x2x4 slice. The times are simulated.
32 devices in a mesh: parts: 2 (over y), tile: 4 (over z), slab: 4 (over x, core).
Axes of the slice: x: 2, y: 2, z: 4, core: 2. Of those that a mesh axis runs over, the one named last changes fastest.
Arguments:
- amps: bfloat16 [4, 32, 64, 64, 512], P('slab', 'tile', None, 'parts'), parts along dimension 3, may hold values from -6 to 6
- integrals: bfloat16 [4, 2048, 2, 2048], P('slab', None, 'parts'), parts along dimension 2, may hold values from -0.09375 to 0.09375
- tile_mask: int32 [4, 64, 32], P('slab', 'parts'), parts along dimension 1, may hold values from 0 to 1, as said below
- amp_map: int32 [32], replicated, may hold values from 0 to 31, each once
- con_map: int32 [32], replicated, may hold values from 0 to 31, each once
Outputs:
- residual: bfloat16 [2048, 2, 32, 512], P('slab', 'parts', 'tile'), parts along dimension 1
There are 2 independent parts, one for each index of `parts`. A program takes and returns all parts, laid end to end along the dimension named above; an argument that names none is the same for every part. Nothing has to cross between parts.
Inputs may be any that keep to these rules, and one draw needn't show every extreme that they name: `tile_mask`: each row (a k tile and an a tile) has between half of 24 and 24 ones, and each k tile has a row with exactly 24. `amp_map`: a permutation of the virtual tiles. `con_map`: a permutation of the virtual tiles.
All inputs are finite; a program needn't handle non-finite values.
Results may differ from a plain program's by a relative error of at most 0.001.
Values may be sent and summed in bfloat16 or wider, within the bound.
A program may use at most 192 MiB of HBM per device.

v0:
```python
import jax
import jax.numpy as jnp
from jax import lax
from jax.sharding import PartitionSpec as P


def local(amps, integrals, tile_mask, amp_map, con_map):
    kcount = amps.shape[0]
    per_dev = amps.shape[1]
    row_width = amps.shape[4]
    virtual = integrals.shape[1]
    jcount = integrals.shape[2]
    position = lax.axis_index("tile")
    offset = position * per_dev
    held_tiles = lax.dynamic_slice(amp_map, (offset,), (per_dev,))
    mask_here = tile_mask[0]
    keeper = jnp.transpose(jnp.take(mask_here, held_tiles, axis=1)).astype(jnp.bfloat16)
    masked = amps * keeper[None, :, None, :, None]
    ordered = jnp.take(masked, con_map, axis=3)
    arrived = lax.all_to_all(ordered, "tile", split_axis=3, concat_axis=1, tiled=True)
    natural = jnp.take(arrived, jnp.argsort(amp_map), axis=1)
    factor_w = integrals.reshape(kcount, virtual * jcount, virtual)
    factor_t = natural.reshape(kcount, virtual, per_dev * row_width)
    summed = jnp.dot(factor_w[0], factor_t[0], preferred_element_type=jnp.float32)
    partial_terms = summed.reshape(virtual, jcount, per_dev, row_width)
    residual_out = lax.psum_scatter(partial_terms, "slab", scatter_dimension=0, tiled=True)
    return residual_out.astype(jnp.bfloat16)


def solution(mesh):
    in_specs = (
        P("slab", "tile", None, "parts", None),
        P("slab", None, "parts", None),
        P("slab", "parts", None),
        P(),
        P(),
    )
    out_specs = P("slab", "parts", "tile", None)
    return jax.shard_map(local, mesh=mesh, in_specs=in_specs, out_specs=out_specs, check_vma=False)
```

profile of v0, /device:TPU:15, one launch (start us, length us, event | category | flops | bytes accessed | tf_op | source)
XLA Modules:
  0.0 815.0 jit_solution(522236220170149121)
XLA Ops:
  6.5 0.7 compare_and_fusion.1
  7.2 0.7 compare_select_fusion.1
  7.9 0.7 compare_and_fusion
  8.6 0.8 copy.16
  9.4 0.6 gather_fusion
  10.0 0.1 select_convert_fusion
  10.0 28.5 %fusion.1 = bf16[8,64,32,512]{3,1,2,0:T(8,128)(2,1)} fusion(bf16[1,8,64,32,512]{4,3,2,1,0:T(8,128)(2,1)} %param.5, bf16[8,32]{1,0:T(8,128)(2,1)S(1)} %select_convert_fusion), kind=kLoop, calls=%fused_computation.8 | loop fusion | flops 8388608 | bytes 33554944 | tf_op jit(solution)/shard_map/mul | solution.py:18
  38.5 13.0 %gather_fusion.1 = bf16[32,8,64,512]{3,2,1,0:T(8,128)(2,1)} fusion(bf16[8,64,32,512]{3,1,2,0:T(8,128)(2,1)} %fusion.1, s32[1024]{0:T(1024)S(1)} %pad_clamp_fusion.1), kind=kCustom, calls=%fused_computation.1 | custom fusion | bytes 33554560 | tf_op jit(solution)/shard_map/jit(_take)/gather | solution.py:19
  51.6 14.2 %fusion = bf16[1,8,64,32,512]{4,2,1,0,3:T(8,128)(2,1)} fusion(bf16[32,8,64,512]{3,2,1,0:T(8,128)(2,1)} %gather_fusion.1, pred[32]{0:T(512)(128)(4,1)S(1)} %compare_and_fusion.1), kind=kLoop, calls=%fused_computation.4 | loop fusion | flops 8388608 | bytes 33554464 | tf_op jit(solution)/shard_map/jit(_take)/select_n | solution.py:19
  65.7 0.0 copy-start
  65.7 7.2 all-to-all-start
  73.0 0.0 reduce-scatter.2.cloned.1.call-start
  73.0 0.0 copy-done
  73.0 1.6 sort.17
  74.6 357.6 %all-to-all-done = bf16[1,8,64,32,512]{4,2,1,0,3:T(8,128)(2,1)} async-done(((bf16[1,8,64,32,512]{4,2,1,0,3:T(8,128)(2,1)}), bf16[1,8,64,32,512]{4,2,1,0,3:T(8,128)(2,1)}, u32[]{:S(2)}, u32[]{:S(2)}) %all-to-all-start) | async-done | bytes 16777248 | tf_op jit(solution)/shard_map/all_to_all | solution.py:20
  432.2 15.5 %copy.27 = bf16[1,8,64,32,512]{4,3,2,1,0:T(8,128)(2,1)S(1)} copy(bf16[1,8,64,32,512]{4,2,1,0,3:T(8,128)(2,1)} %all-to-all-done) | data formatting | bytes 33554432 | tf_op jit(solution)/shard_map/all_to_all | solution.py:20
  447.6 7.5 copy.20
  455.1 13.0 %gather_fusion.2 = bf16[32,64,8,512]{3,2,1,0:T(8,128)(2,1)} fusion(bf16[32,64,8,512]{3,2,1,0:T(8,128)(2,1)} %bitcast.29, s32[1024]{0:T(1024)S(1)} %pad_clamp_fusion), kind=kCustom, calls=%fused_computation.2 | custom fusion | bytes 33554560 | tf_op jit(solution)/shard_map/jit(_take)/gather | solution.py:21
  468.2 8.5 %bitcast_select_fusion.1 = bf16[1,32,64,8,512]{4,3,2,1,0:T(8,128)(2,1)S(1)} fusion(bf16[32,64,8,512]{3,2,1,0:T(8,128)(2,1)} %gather_fusion.2, pred[32]{0:T(512)(128)(4,1)S(1)} %compare_and_fusion.2), kind=kLoop, calls=%fused_computation.5 | loop fusion | flops 8388608 | bytes 33554464 | tf_op jit(solution)/shard_map/jit(_take)/select_n | solution.py:21
  476.7 10.4 %copy.22 = bf16[256,8,8,512]{3,1,2,0:T(8,128)(2,1)} copy(bf16[256,8,8,512]{3,2,1,0:T(8,128)(2,1)S(1)} %bitcast.30) | data formatting | bytes 33554432
  487.1 43.4 %fusion.2 = f32[4096,2048]{1,0:T(8,128)} fusion(bf16[2048,4096]{1,0:T(8,128)(2,1)} %bitcast.33, bf16[1,2048,1,2048]{3,1,2,0:T(8,128)(2,1)} %param.6), kind=kOutput, calls=%fused_computation.9 | convolution fusion | flops 34359738368 | bytes 58720256 | tf_op jit(solution)/shard_map/dot_general | solution.py:24
  530.5 34.8 %copy.21 = f32[2048,1,8,512]{3,2,1,0:T(8,128)} copy(f32[2048,1,8,512]{0,3,2,1:T(8,128)} %bitcast.32) | data formatting | bytes 67108864 | tf_op jit(solution)/shard_map/reshape | solution.py:25
  565.3 0.0 reduce-scatter.2.cloned.1.call-update
  565.3 236.9 %reduce-scatter.2.cloned.1.call-done = f32[512,1,8,512]{3,2,1,0:T(8,128)} async-done(((f32[2048,1,8,512]{3,2,1,0:T(8,128)}), f32[512,1,8,512]{3,2,1,0:T(8,128)}) %reduce-scatter.2.cloned.1.call-update) | async-done | bytes 8388624 | tf_op jit(solution)/shard_map/reduce_scatter | solution.py:26
  802.2 5.9 convert_element_type.11
  (6 shorter events, 0.0 us)
Async XLA Ops:
  65.7 7.2 copy-start
  65.7 366.4 %all-to-all-start = ((bf16[1,8,64,32,512]{4,2,1,0,3:T(8,128)(2,1)}), bf16[1,8,64,32,512]{4,2,1,0,3:T(8,128)(2,1)}, u32[]{:S(2)}, u32[]{:S(2)}) async-start(bf16[1,8,64,32,512]{4,2,1,0,3:T(8,128)(2,1)} %fusion), calls=%async_computation | async-start | bytes 33554432 | tf_op jit(solution)/shard_map/all_to_all | solution.py:20
  73.0 729.2 %reduce-scatter.2.cloned.1.call-start = ((), (), s32[]{:S(2)}) async-start(), calls=%async_computation.2 | async-start | bytes 41943040 | tf_op jit(solution)/shard_map/reduce_scatter | solution.py:26
Sparse Core Ops, SparseCore 0:
  565.5 236.6 reduce-scatter.1
where the time goes:
time: 818 us; the launch traced here: 815 us
  waiting for transfers between devices  594 us (73%)
  local copies, waits for them, and re-layouts  95.6 us (12%)
  other arithmetic  60.9 us (7%)
  matrix products  43.4 us (5%)
  between operations  13.4 us (2%)
    all_to_all x1, waiting for transfers between devices, local(): lax.all_to_all(ordered, 'tile', split_axis=3, concat_axis=1, tiled=True)  358 us
    reduce_scatter x1, waiting for transfers between devices, local(): lax.psum_scatter(partial_terms, 'slab', scatter_dimension=0, tiled=True)  237 us
    dot_general x1, matrix products, local(): jnp.dot(factor_w[0], factor_t[0], preferred_element_type=jnp.float32)  43.4 us
    reshape x1, local copies, waits for them, and re-layouts, local(): partial_terms = summed.reshape(virtual, jcount, per_dev, row_width)  34.8 us
    mul x1, other arithmetic, local(): masked = amps * keeper[None, :, None, :, None]  28.5 us
    all_to_all x2, local copies, waits for them, and re-layouts, local(): lax.all_to_all(ordered, 'tile', split_axis=3, concat_axis=1, tiled=True)  23 us
  transfers between devices with their start and end apart: 2, of which 2 were waited for; matrix products, arithmetic and copies ran while one was open for 0% of the time, Pallas kernels for 0%

commit v1 on v0

v1 whole, which is shorter than its diff:
```python
import functools

import jax
import jax.numpy as jnp
from jax import lax
from jax.experimental import pallas as pl
from jax.experimental.pallas import tpu as pltpu
from jax.sharding import PartitionSpec as P

MESH = pl.DeviceIdType.MESH
GROUP = 16
CHUNK = 256
AHEAD = 2


def arrange(nvt, ts, width, target_ref, amps_ref, out_ref):
    rows = GROUP * nvt
    column = lax.broadcasted_iota(jnp.int32, (rows, rows), 1)
    select = jnp.where(column == target_ref[0], 1.0, 0.0).astype(jnp.bfloat16)
    for part in range(ts // GROUP):
        block = amps_ref[pl.ds(part * rows, rows), :]
        moved = jnp.dot(select, block, preferred_element_type=jnp.float32)
        moved = moved.astype(jnp.bfloat16).reshape(nvt, GROUP, width)
        out_ref[:, 0, pl.ds(part * GROUP, GROUP), :] = moved


def contract(n_tile, per_dev, nvt, ts, width,
             column_ref, sent_ref, w_ref, out_ref,
             tiles, w_raw, w_held, give1, got1, keep, give2, got2,
             tile_send, tile_recv, own_sem, w_sem,
             send1, recv1, send2, recv2):
    me = lax.axis_index("tile")
    slab = lax.axis_index("slab")
    near = slab + 1 - 2 * (slab % 2)
    far = (slab + 2) % 4
    cross = (near + 2) % 4
    rows = out_ref.shape[1]
    count = per_dev
    depth = per_dev * ts
    virtual = nvt * ts

    def tile_copy(q, step):
        there = (me + step) % n_tile
        return pltpu.make_async_remote_copy(
            src_ref=sent_ref.at[there * per_dev + q],
            dst_ref=tiles.at[q, pl.ds(me * depth, depth)],
            send_sem=tile_send.at[q, step],
            recv_sem=tile_recv.at[q, me],
            device_id={"tile": there},
            device_id_type=MESH,
        )

    def tile_arrival(q, step):
        source = (me + step) % n_tile
        return pltpu.make_async_remote_copy(
            src_ref=sent_ref.at[q],
            dst_ref=tiles.at[q, pl.ds(source * depth, depth)],
            send_sem=tile_send.at[q, step],
            recv_sem=tile_recv.at[q, source],
            device_id={"tile": source},
            device_id_type=MESH,
        )

    def own_copy(q):
        return pltpu.make_async_copy(
            sent_ref.at[me * per_dev + q],
            tiles.at[q, pl.ds(me * depth, depth)],
            own_sem.at[q],
        )

    def copy1(slot):
        return pltpu.make_async_remote_copy(
            src_ref=give1.at[slot], dst_ref=got1.at[slot],
            send_sem=send1.at[slot], recv_sem=recv1.at[slot],
            device_id={"slab": near}, device_id_type=MESH,
        )

    def copy2(slot):
        return pltpu.make_async_remote_copy(
            src_ref=give2.at[slot], dst_ref=got2.at[slot],
            send_sem=send2.at[slot], recv_sem=recv2.at[slot],
            device_id={"slab": far}, device_id_type=MESH,
        )

    w_copy = pltpu.make_async_copy(w_ref, w_raw, w_sem)

    barrier = pltpu.get_barrier_semaphore()
    for step in range(1, n_tile):
        pl.semaphore_signal(barrier, inc=1, device_id={"tile": (me + step) % n_tile}, device_id_type=MESH)
    pl.semaphore_signal(barrier, inc=1, device_id={"slab": near}, device_id_type=MESH)
    pl.semaphore_signal(barrier, inc=1, device_id={"slab": far}, device_id_type=MESH)
    pl.semaphore_wait(barrier, n_tile + 1)

    def send_tiles(q):
        for step in range(1, n_tile):
            tile_copy(q, step).start()

    for q in range(min(AHEAD, count)):
        send_tiles(q)
    w_copy.start()
    for q in range(count):
        own_copy(q).start()
    w_copy.wait()

    def reorder(chunk, carry):
        here = pl.ds(pl.multiple_of(chunk * CHUNK, CHUNK), CHUNK)
        line = lax.broadcasted_iota(jnp.int32, (virtual, CHUNK), 0)
        select = jnp.where(line == column_ref[:, here], 1.0, 0.0).astype(jnp.bfloat16)
        for block in range(virtual // rows):
            span = pl.ds(block * rows, rows)
            w_held[span, here] = jnp.dot(
                w_raw[span, :], select, preferred_element_type=jnp.float32
            ).astype(jnp.bfloat16)
        return carry

    lax.fori_loop(0, virtual // CHUNK, reorder, 0)

    def product(q, block):
        return jnp.dot(w_held[pl.ds(pl.multiple_of(block * rows, rows), rows), :], tiles[q],
                       preferred_element_type=jnp.float32)

    def finish(q, slot):
        copy2(slot).wait_recv()
        out_ref[q] = (keep[slot] + got2[slot]).astype(jnp.bfloat16)

    def step(q, carry):
        slot = q % 2
        own_copy(q).wait()
        for other in range(1, n_tile):
            tile_arrival(q, other).wait_recv()

        @pl.when(q + AHEAD < count)
        def _():
            send_tiles(q + AHEAD)

        @pl.when(q >= 2)
        def _():
            copy1(slot).wait_send()

        give1[slot, 0] = product(q, near)
        give1[slot, 1] = product(q, cross)
        copy1(slot).start()

        @pl.when(q >= 1)
        def _():
            finish(q - 1, 1 - slot)

        @pl.when(q >= 2)
        def _():
            copy2(slot).wait_send()

        give2[slot] = product(q, far)
        keep[slot] = product(q, slab)
        copy1(slot).wait_recv()
        give2[slot] = give2[slot] + got1[slot, 1]
        copy2(slot).start()
        keep[slot] = keep[slot] + got1[slot, 0]
        for other in range(1, n_tile):
            tile_copy(q, other).wait_send()
        return carry

    lax.fori_loop(0, count, step, 0)
    finish(count - 1, (count - 1) % 2)
    for q in range(max(count - 2, 0), count):
        copy1(q % 2).wait_send()
        copy2(q % 2).wait_send()


def local(n_tile, n_slab, amps, integrals, tile_mask, amp_map, con_map):
    per_dev, ts, nvt, width = amps.shape[1:]
    virtual = integrals.shape[1]
    rows = virtual // n_slab
    position = lax.axis_index("tile")
    held = lax.dynamic_slice(amp_map, (position * per_dev,), (per_dev,))
    column = (amp_map[:, None] * ts + jnp.arange(ts, dtype=jnp.int32)).reshape(1, virtual)
    alive = jnp.take(jnp.take(tile_mask[0], con_map, axis=0), held, axis=1).T
    shift = nvt * jnp.arange(GROUP, dtype=jnp.int32)
    target = jnp.where(alive[:, :, None] != 0, con_map[None, :, None] + shift, -1)
    target = target.reshape(per_dev, nvt * GROUP, 1).astype(jnp.int32)

    flat = amps.reshape(per_dev * ts * nvt, width)
    ordered = pl.pallas_call(
        functools.partial(arrange, nvt, ts, width),
        grid=(per_dev,),
        out_shape=jax.ShapeDtypeStruct((nvt, per_dev, ts, width), jnp.bfloat16),
        in_specs=[
            pl.BlockSpec((1, nvt * GROUP, 1), lambda p: (p, 0, 0)),
            pl.BlockSpec((ts * nvt, width), lambda p: (p, 0)),
        ],
        out_specs=pl.BlockSpec((nvt, 1, ts, width), lambda p: (0, p, 0, 0)),
        compiler_params=pltpu.CompilerParams(vmem_limit_bytes=40 * 2**20),
    )(target, flat)

    summed = pl.pallas_call(
        functools.partial(contract, n_tile, per_dev, nvt, ts, width),
        out_shape=jax.ShapeDtypeStruct((per_dev, rows, width), jnp.bfloat16),
        in_specs=[
            pl.BlockSpec(memory_space=pltpu.VMEM),
            pl.BlockSpec(memory_space=pl.ANY),
            pl.BlockSpec(memory_space=pl.ANY),
        ],
        out_specs=pl.BlockSpec(memory_space=pltpu.VMEM),
        scratch_shapes=[
            pltpu.VMEM((per_dev, virtual, width), jnp.bfloat16),
            pltpu.VMEM((virtual, virtual), jnp.bfloat16),
            pltpu.VMEM((virtual, virtual), jnp.bfloat16),
            pltpu.VMEM((2, 2, rows, width), jnp.float32),
            pltpu.VMEM((2, 2, rows, width), jnp.float32),
            pltpu.VMEM((2, rows, width), jnp.float32),
            pltpu.VMEM((2, rows, width), jnp.float32),
            pltpu.VMEM((2, rows, width), jnp.float32),
            pltpu.SemaphoreType.DMA((per_dev, n_tile)),
            pltpu.SemaphoreType.DMA((per_dev, n_tile)),
            pltpu.SemaphoreType.DMA((per_dev,)),
            pltpu.SemaphoreType.DMA,
            pltpu.SemaphoreType.DMA((2,)),
            pltpu.SemaphoreType.DMA((2,)),
            pltpu.SemaphoreType.DMA((2,)),
            pltpu.SemaphoreType.DMA((2,)),
        ],
        compiler_params=pltpu.CompilerParams(
            collective_id=0, has_side_effects=True, vmem_limit_bytes=58 * 2**20
        ),
    )(column.astype(jnp.int32), ordered.reshape(nvt, per_dev * ts, width), integrals.reshape(virtual, virtual))
    return jnp.transpose(summed, (1, 0, 2))[:, None]


def solution(mesh):
    in_specs = (
        P("slab", "tile", None, "parts", None),
        P("slab", None, "parts", None),
        P("slab", "parts", None),
        P(),
        P(),
    )
    out_specs = P("slab", "parts", "tile", None)
    body = functools.partial(local, mesh.shape["tile"], mesh.shape["slab"])
    return jax.shard_map(body, mesh=mesh, in_specs=in_specs, out_specs=out_specs, check_vma=False)
```

time: 818 us -> 434 us (0.53)
  waiting for transfers between devices: 594 us -> 0 us
  Pallas kernels: 0 us -> 419 us
  local copies, waits for them, and re-layouts: 95.6 us -> 11.3 us
  other arithmetic: 60.9 us -> 3.3 us
  matrix products: 43.4 us -> 0 us
  between operations: 13.4 us -> 0.06 us
    pallas_call x0 -> x2, Pallas kernels: none -> 419 us  [the longest x1 402 us: local(): pl.pallas_call(functools.partial(contract, n_tile, per_dev, nvt, ts, widt...]
    all_to_all x1 -> x0, waiting for transfers between devices: 358 us -> none  [local(): lax.all_to_all(ordered, 'tile', split_axis=3, concat_axis=1, tiled=True)]
    reduce_scatter x1 -> x0, waiting for transfers between devices: 237 us -> none  [local(): lax.psum_scatter(partial_terms, 'slab', scatter_dimension=0, tiled=True)]
    dot_general x1 -> x0, matrix products: 43.4 us -> none  [local(): jnp.dot(factor_w[0], factor_t[0], preferred_element_type=jnp.float32)]
    reshape x1 -> x0, local copies, waits for them, and re-layouts: 34.8 us -> none  [local(): partial_terms = summed.reshape(virtual, jcount, per_dev, row_width)]
    mul x1 -> x2, other arithmetic: 28.5 us -> 0.66 us  [the longest x1 0.66 us: local(): amp_map[:, None] * ts + jnp.arange(ts, dtype=jnp.int32)]
    gather x3 -> x2, local copies, waits for them, and re-layouts: 26.6 us -> 1.13 us  [local(): alive = jnp.take(jnp.take(tile_mask[0], con_map, axis=0), held, axis=1).T]
    all_to_all x2 -> x0, local copies, waits for them, and re-layouts: 23 us -> none  [local(): lax.all_to_all(ordered, 'tile', split_axis=3, concat_axis=1, tiled=True)]
  transfers between devices with their start and end apart: 2 -> 0, of which waited for: 2 -> 0; matrix products, arithmetic and copies ran while one was open for 0% -> 0% of each run, Pallas kernels for 0% -> 0%
where the time goes in v1:
time: 434 us
  Pallas kernels  419 us (97%)
  local copies, waits for them, and re-layouts  11.3 us (3%)
    pallas_call x1, Pallas kernels, local(): pl.pallas_call(functools.partial(contract, n_tile, per_dev, nvt, ts, widt...  402 us
    pallas_call x1, Pallas kernels, local(): pl.pallas_call(functools.partial(arrange, nvt, ts, width), grid=(per_dev,...  17 us

profile of v1, /device:TPU:15, one launch (start us, length us, event | category | flops | bytes accessed | tf_op | source)
XLA Modules:
  0.0 433.8 jit_solution(16041450180656707697)
XLA Ops:
  0.0 0.0 copy-start
  0.0 0.7 copy-done
  0.7 0.7 broadcast_multiply_fusion
  1.4 0.7 compare_and_fusion
  2.0 0.7 compare_select_fusion
  2.7 0.7 compare_and_fusion.1
  3.5 0.6 gather_fusion
  4.0 0.1 broadcast_select_fusion.1
  4.1 0.1 copy.8
  4.2 0.6 gather_fusion.1
  4.7 0.1 select_compare_fusion
  4.8 0.1 add.71
  4.9 0.1 iota_add_fusion
  5.0 0.7 add.63.column_ref
  5.7 0.7 add.68
  6.4 0.1 add.69
  6.5 0.1 broadcast_in_dim.60
  6.6 1.2 broadcast_in_dim.65
  7.8 0.4 broadcast_select_fusion.target_ref
  8.2 17.0 %shard_map.55 = bf16[32,8,64,512]{3,2,1,0:T(8,128)(2,1)} custom-call(s32[8,512,1]{2,1,0:T(8,128)S(1)} %broadcast_select_fusion.target_ref, bf16[16384,512]{1,0:T(8,128)(2,1)} %bitcast.11), custom_call_target="tpu_custom_call" | custom-call | tf_op jit(solution)/shard_map/pallas_call | solution.py:182
  25.1 402.1 %shard_map.56 = bf16[8,512,512]{2,1,0:T(8,128)(2,1)} custom-call(s32[1,2048]{1,0:T(1,128)} %add.63.column_ref, bf16[32,512,512]{2,1,0:T(8,128)(2,1)} %bitcast.10, bf16[2048,2048]{1,0:T(8,128)(2,1)} %bitcast.13), custom_call_target="tpu_custom_call" | custom-call | tf_op jit(solution)/shard_map/pallas_call | solution.py:194
  427.3 6.5 %copy.10 = bf16[512,1,8,512]{3,2,1,0:T(8,128)(2,1)} copy(bf16[512,1,8,512]{3,0,2,1:T(8,128)(2,1)} %bitcast.12) | data formatting | bytes 8388608 | tf_op jit(solution)/shard_map/broadcast_in_dim | solution.py:225
  (5 shorter events, 0.0 us)
Async XLA Ops:
  0.0 0.7 copy-start

commit v2 on v1

v2 whole, which is shorter than its diff:
```python
import functools

import jax
import jax.numpy as jnp
from jax import lax
from jax.experimental import pallas as pl
from jax.experimental.pallas import tpu as pltpu
from jax.sharding import PartitionSpec as P

MESH = pl.DeviceIdType.MESH
GROUP = 16
CHUNK = 256
SPLIT = 2
EARLY = 2
AHEAD = 4


def contract(n_tile, per_dev, nvt, ts, width,
             mask_ref, amp_ref, con_ref, amps_ref, w_ref, out_ref, sent_ref,
             blocks, select, stage, tiles, w_raw, w_held, give1, got1, keep, give2, got2,
             in_sem, stage_sem, tile_send, tile_recv, own_sem, w_sem,
             send1, recv1, send2, recv2):
    me = lax.axis_index("tile")
    slab = lax.axis_index("slab")
    near = slab + 1 - 2 * (slab % 2)
    far = (slab + 2) % 4
    cross = (near + 2) % 4
    rows = out_ref.shape[1]
    piece = width // SPLIT
    count = per_dev * SPLIT
    depth = per_dev * ts
    virtual = nvt * ts
    early = min(EARLY, count)

    def tile_copy(u, step, start=0, size=depth):
        there = (me + step) % n_tile
        return pltpu.make_async_remote_copy(
            src_ref=sent_ref.at[there * per_dev + u // SPLIT, u % SPLIT, pl.ds(start, size)],
            dst_ref=tiles.at[u, pl.ds(me * depth + start, size)],
            send_sem=tile_send.at[u, step],
            recv_sem=tile_recv.at[u, me],
            device_id={"tile": there},
            device_id_type=MESH,
        )

    def tile_arrival(u, step):
        source = (me + step) % n_tile
        return pltpu.make_async_remote_copy(
            src_ref=sent_ref.at[u // SPLIT, u % SPLIT],
            dst_ref=tiles.at[u, pl.ds(source * depth, depth)],
            send_sem=tile_send.at[u, step],
            recv_sem=tile_recv.at[u, source],
            device_id={"tile": source},
            device_id_type=MESH,
        )

    def own_copy(u):
        return pltpu.make_async_copy(
            sent_ref.at[me * per_dev + u // SPLIT, u % SPLIT],
            tiles.at[u, pl.ds(me * depth, depth)],
            own_sem.at[u],
        )

    def copy1(slot):
        return pltpu.make_async_remote_copy(
            src_ref=give1.at[slot], dst_ref=got1.at[slot],
            send_sem=send1.at[slot], recv_sem=recv1.at[slot],
            device_id={"slab": near}, device_id_type=MESH,
        )

    def copy2(slot):
        return pltpu.make_async_remote_copy(
            src_ref=give2.at[slot], dst_ref=got2.at[slot],
            send_sem=send2.at[slot], recv_sem=recv2.at[slot],
            device_id={"slab": far}, device_id_type=MESH,
        )

    def in_copy(p, slot):
        return pltpu.make_async_copy(
            amps_ref.at[pl.ds(p * virtual, virtual)], blocks.at[slot], in_sem.at[slot]
        )

    def stage_copy(p, slot):
        return pltpu.make_async_copy(
            stage.at[slot], sent_ref.at[:, :, pl.ds(p * ts, ts), :], stage_sem.at[slot]
        )

    w_copy = pltpu.make_async_copy(w_ref, w_raw, w_sem)

    barrier = pltpu.get_barrier_semaphore()
    for step in range(1, n_tile):
        pl.semaphore_signal(barrier, inc=1, device_id={"tile": (me + step) % n_tile}, device_id_type=MESH)
    pl.semaphore_signal(barrier, inc=1, device_id={"slab": near}, device_id_type=MESH)
    pl.semaphore_signal(barrier, inc=1, device_id={"slab": far}, device_id_type=MESH)
    in_copy(0, 0).start()
    w_copy.start()
    pl.semaphore_wait(barrier, n_tile + 1)

    def first_sends(p):
        for u in range(early):
            for step in range(1, n_tile):
                tile_copy(u, step, p * ts, ts).start()

    size = GROUP * nvt
    offset = (lax.broadcasted_iota(jnp.int32, (GROUP, size), 1)
              - nvt * lax.broadcasted_iota(jnp.int32, (GROUP, size), 0))

    def arrange(p, carry):
        slot = p % 2

        @pl.when(p + 1 < per_dev)
        def _():
            in_copy(p + 1, 1 - slot).start()

        c_tile = amp_ref[me * per_dev + p]

        def choose(q, inner):
            a_tile = con_ref[q]
            wanted = jnp.where(mask_ref[a_tile, c_tile] != 0, a_tile, -2 * size)
            select[pl.ds(pl.multiple_of(q * GROUP, GROUP), GROUP), :] = jnp.where(
                offset == wanted, 1.0, 0.0).astype(jnp.bfloat16)
            return inner

        lax.fori_loop(0, nvt, choose, 0)
        in_copy(p, slot).wait()
        for part in range(ts // GROUP):
            moved = jnp.dot(select[...], blocks[slot, pl.ds(part * size, size), :],
                            preferred_element_type=jnp.float32)
            moved = moved.astype(jnp.bfloat16).reshape(nvt, GROUP, width)
            for h in range(SPLIT):
                stage[slot, :, h, pl.ds(part * GROUP, GROUP), :] = moved[:, :, h * piece:(h + 1) * piece]
        stage_copy(p, slot).start()

        @pl.when(p >= 1)
        def _():
            stage_copy(p - 1, 1 - slot).wait()
            first_sends(p - 1)

        return carry

    lax.fori_loop(0, per_dev, arrange, 0)
    stage_copy(per_dev - 1, (per_dev - 1) % 2).wait()
    first_sends(per_dev - 1)

    def send_tiles(u):
        for step in range(1, n_tile):
            tile_copy(u, step).start()

    for u in range(early, min(AHEAD, count)):
        send_tiles(u)
    for u in range(count):
        own_copy(u).start()
    w_copy.wait()

    def reorder(chunk, carry):
        here = pl.ds(pl.multiple_of(chunk * CHUNK, CHUNK), CHUNK)
        lane = lax.broadcasted_iota(jnp.int32, (1, CHUNK), 1)
        wanted = lane % ts
        for j in range(CHUNK // ts):
            wanted = wanted + jnp.where(lane // ts == j, amp_ref[chunk * (CHUNK // ts) + j] * ts, 0)
        line = lax.broadcasted_iota(jnp.int32, (virtual, CHUNK), 0)
        pick = jnp.where(line == wanted, 1.0, 0.0).astype(jnp.bfloat16)
        for block in range(virtual // rows):
            span = pl.ds(block * rows, rows)
            w_held[span, here] = jnp.dot(
                w_raw[span, :], pick, preferred_element_type=jnp.float32
            ).astype(jnp.bfloat16)
        return carry

    lax.fori_loop(0, virtual // CHUNK, reorder, 0)

    def product(u, block):
        return jnp.dot(w_held[pl.ds(pl.multiple_of(block * rows, rows), rows), :], tiles[u],
                       preferred_element_type=jnp.float32)

    def finish(u, slot):
        copy2(slot).wait_recv()
        lanes = pl.ds(pl.multiple_of((u % SPLIT) * piece, piece), piece)
        out_ref[u // SPLIT, :, lanes] = (keep[slot] + got2[slot]).astype(jnp.bfloat16)

    def step(u, carry):
        slot = u % 2
        own_copy(u).wait()
        for other in range(1, n_tile):
            tile_arrival(u, other).wait_recv()

        @pl.when(u + AHEAD < count)
        def _():
            send_tiles(u + AHEAD)

        @pl.when(u >= 2)
        def _():
            copy1(slot).wait_send()

        give1[slot, 0] = product(u, near)
        give1[slot, 1] = product(u, cross)
        copy1(slot).start()

        @pl.when(u >= 1)
        def _():
            finish(u - 1, 1 - slot)

        @pl.when(u >= 2)
        def _():
            copy2(slot).wait_send()

        give2[slot] = product(u, far)
        keep[slot] = product(u, slab)
        copy1(slot).wait_recv()
        give2[slot] = give2[slot] + got1[slot, 1]
        copy2(slot).start()
        keep[slot] = keep[slot] + got1[slot, 0]
        for other in range(1, n_tile):
            tile_copy(u, other).wait_send()
        return carry

    lax.fori_loop(0, count, step, 0)
    finish(count - 1, (count - 1) % 2)
    for u in range(max(count - 2, 0), count):
        copy1(u % 2).wait_send()
        copy2(u % 2).wait_send()


def local(n_tile, n_slab, amps, integrals, tile_mask, amp_map, con_map):
    per_dev, ts, nvt, width = amps.shape[1:]
    virtual = integrals.shape[1]
    rows = virtual // n_slab
    piece = width // SPLIT
    count = per_dev * SPLIT
    summed, sent = pl.pallas_call(
        functools.partial(contract, n_tile, per_dev, nvt, ts, width),
        out_shape=(
            jax.ShapeDtypeStruct((per_dev, rows, width), jnp.bfloat16),
            jax.ShapeDtypeStruct((nvt, SPLIT, per_dev * ts, piece), jnp.bfloat16),
        ),
        in_specs=[
            pl.BlockSpec(memory_space=pltpu.SMEM),
            pl.BlockSpec(memory_space=pltpu.SMEM),
            pl.BlockSpec(memory_space=pltpu.SMEM),
            pl.BlockSpec(memory_space=pl.ANY),
            pl.BlockSpec(memory_space=pl.ANY),
        ],
        out_specs=(
            pl.BlockSpec(memory_space=pltpu.VMEM),
            pl.BlockSpec(memory_space=pl.ANY),
        ),
        scratch_shapes=[
            pltpu.VMEM((2, virtual, width), jnp.bfloat16),
            pltpu.VMEM((nvt * GROUP, nvt * GROUP), jnp.bfloat16),
            pltpu.VMEM((2, nvt, SPLIT, ts, piece), jnp.bfloat16),
            pltpu.VMEM((count, virtual, piece), jnp.bfloat16),
            pltpu.VMEM((virtual, virtual), jnp.bfloat16),
            pltpu.VMEM((virtual, virtual), jnp.bfloat16),
            pltpu.VMEM((2, 2, rows, piece), jnp.float32),
            pltpu.VMEM((2, 2, rows, piece), jnp.float32),
            pltpu.VMEM((2, rows, piece), jnp.float32),
            pltpu.VMEM((2, rows, piece), jnp.float32),
            pltpu.VMEM((2, rows, piece), jnp.float32),
            pltpu.SemaphoreType.DMA((2,)),
            pltpu.SemaphoreType.DMA((2,)),
            pltpu.SemaphoreType.DMA((count, n_tile)),
            pltpu.SemaphoreType.DMA((count, n_tile)),
            pltpu.SemaphoreType.DMA((count,)),
            pltpu.SemaphoreType.DMA,
            pltpu.SemaphoreType.DMA((2,)),
            pltpu.SemaphoreType.DMA((2,)),
            pltpu.SemaphoreType.DMA((2,)),
            pltpu.SemaphoreType.DMA((2,)),
        ],
        compiler_params=pltpu.CompilerParams(
            collective_id=0, has_side_effects=True, vmem_limit_bytes=60 * 2**20
        ),
    )(tile_mask[0], amp_map, con_map, amps.reshape(per_dev * virtual, width),
      integrals.reshape(virtual, virtual))
    return jnp.transpose(summed, (1, 0, 2))[:, None]


def solution(mesh):
    in_specs = (
        P("slab", "tile", None, "parts", None),
        P("slab", None, "parts", None),
        P("slab", "parts", None),
        P(),
        P(),
    )
    out_specs = P("slab", "parts", "tile", None)
    body = functools.partial(local, mesh.shape["tile"], mesh.shape["slab"])
    return jax.shard_map(body, mesh=mesh, in_specs=in_specs, out_specs=out_specs, check_vma=False)
```

time: 434 us -> 407 us (0.938)
  Pallas kernels: 419 us -> 400 us
  local copies, waits for them, and re-layouts: 11.3 us -> 6.54 us
    pallas_call x1 -> x0, Pallas kernels: 17 us -> none  [local(): pl.pallas_call(functools.partial(arrange, nvt, ts, width), grid=(per_dev,...]
where the time goes in v2:
time: 407 us; the launch traced here: 406 us
  Pallas kernels  400 us (98%)
  local copies, waits for them, and re-layouts  6.54 us (2%)
    pallas_call x1, Pallas kernels, local(): pl.pallas_call(functools.partial(contract, n_tile, per_dev, nvt, ts, widt...  400 us

profile of v2, /device:TPU:15, one launch (start us, length us, event | category | flops | bytes accessed | tf_op | source)
XLA Modules:
  0.0 406.2 jit_solution(1882878087308317616)
XLA Ops:
  0.0 399.7 %shard_map.55 = (bf16[8,512,512]{2,1,0:T(8,128)(2,1)}, bf16[32,2,512,256]{3,2,1,0:T(8,128)(2,1)}) custom-call(s32[32,32]{1,0:T(8,128)} %bitcast.9, s32[32]{0:T(128)} %amp_ref.1, s32[32]{0:T(128)} %con_ref.1, bf16[16384,512]{1,0:T(8,128)(2,1)} %bitcast.6, bf16[2048,2048]{1,0:T(8,128)(2,1)} %bitcast.7), custom_call_target="tpu_custom_call" | custom-call | tf_op jit(solution)/shard_map/pallas_call | solution.py:230
  399.7 6.5 %copy.6 = bf16[512,1,8,512]{3,2,1,0:T(8,128)(2,1)} copy(bf16[512,1,8,512]{3,0,2,1:T(8,128)(2,1)} %bitcast.8) | data formatting | bytes 8388608 | tf_op jit(solution)/shard_map/broadcast_in_dim | solution.py:275
